TPU v7x, 32 devices: a whole 2x2x4 slice. The times are simulated.
32 devices in a mesh: groups: 2 (over y), dp: 16 (over z, x, core).
Axes of the slice: x: 2, y: 2, z: 4, core: 2. Of those that a mesh axis runs over, the one named last changes fastest.
Arguments:
- stored_inputs: bfloat16 [64, 128, 14336], P(('groups', 'dp')), parts along dimension 0, may hold values from -6 to 6
- output_grads: bfloat16 [64, 128, 4096], P(('groups', 'dp')), parts along dimension 0, may hold values from -6 to 6
- basis_in: bfloat16 [14336, 64], replicated, may hold values from -0.046875 to 0.046875
- basis_out: bfloat16 [4096, 64], replicated, may hold values from -0.09375 to 0.09375
- ex_weight: float32 [64], P(('groups', 'dp')), parts along dimension 0, may hold values from 0.5 to 18, as said below
Outputs:
- fisher: float32 [8192, 1024], P(('groups', 'dp')), parts along dimension 0
- proj_grads: bfloat16 [64, 4096], P(('groups', 'dp')), parts along dimension 0
There are 2 independent parts, one for each index of `groups`. A program takes and returns all parts, laid end to end along the dimension named above; an argument that names none is the same for every part. Nothing has to cross between parts.
Inputs may be any that keep to these rules, and one draw needn't show every extreme that they name: `ex_weight`: each example's importance weight is positive.
All inputs are finite; a program needn't handle non-finite values.
Results may differ from a plain program's by a relative error of at most 0.0065.
Values sent between devices are 32-bit elements; how exact they have to be, the bound alone decides.
A program may use at most 128 MiB of HBM per device.

v0:
```python
import jax
import jax.numpy as jnp
from jax import lax
from jax.sharding import PartitionSpec as P

FCOLS = 1024


epsilon = 1e-06


def local(stored_inputs, output_grads, basis_in, basis_out, ex_weight):
    ex_count, seq_len, in_width = stored_inputs.shape
    out_width = output_grads.shape[2]
    rank_in = basis_in.shape[1]
    rank_out = basis_out.shape[1]
    proj_width = rank_in * rank_out
    col_count = FCOLS
    proj_in = jnp.dot(
        stored_inputs.reshape(ex_count * seq_len, in_width),
        basis_in,
        preferred_element_type=jnp.float32,
    ).astype(jnp.bfloat16)
    proj_out = jnp.dot(
        output_grads.reshape(ex_count * seq_len, out_width),
        basis_out,
        preferred_element_type=jnp.float32,
    ).astype(jnp.bfloat16)
    proj_in = proj_in.reshape(ex_count, seq_len, rank_in)
    proj_out = proj_out.reshape(ex_count, seq_len, rank_out)
    blocks = jnp.einsum("eto,eti->eoi", proj_out, proj_in, preferred_element_type=jnp.float32)
    flat = blocks.reshape(ex_count, proj_width)
    weighted = flat * ex_weight[:, None]
    left_cols = flat[:, :col_count]
    fisher_rows = lax.psum_scatter(
        jnp.dot(
            weighted.T,
            left_cols,
            precision=lax.Precision.HIGHEST,
            preferred_element_type=jnp.float32,
        ),
        "dp",
        scatter_dimension=0,
        tiled=True,
    )
    trace_total = lax.psum(jnp.sum(weighted * flat), "dp")
    fisher = fisher_rows * (proj_width / (trace_total + epsilon))
    return (fisher, flat.astype(jnp.bfloat16))


def solution(mesh):
    in_specs = (
        P(("groups", "dp"), None, None),
        P(("groups", "dp"), None, None),
        P(),
        P(),
        P(("groups", "dp")),
    )
    out_specs = (P(("groups", "dp"), None), P(("groups", "dp"), None))
    return jax.shard_map(local, mesh=mesh, in_specs=in_specs, out_specs=out_specs, check_vma=False)
```

profile of v0, /device:TPU:0, one launch (start us, length us, event | category | flops | bytes accessed | tf_op | source)
XLA Modules:
  0.0 221.7 jit_solution(17267718423735931859)
XLA Ops:
  7.2 0.0 copy-start
  7.2 0.0 reduce-scatter.2.cloned.1.call-start
  7.2 0.0 copy-start.1
  7.2 6.1 %fusion = bf16[8,2,8,128]{3,2,1,0:T(8,128)(2,1)S(1)} fusion(bf16[256,14336]{1,0:T(8,128)(2,1)} %bitcast.21, bf16[14336,64]{0,1:T(8,128)(2,1)} %param.7), kind=kOutput, calls=%fused_computation.2 | convolution fusion | flops 469778432 | bytes 9207808 | tf_op jit(solution)/shard_map/dot_general | solution.py:19
  13.3 0.0 copy-done
  13.3 0.0 copy-start.2
  13.3 0.0 copy-done.1
  13.3 0.8 fusion.1
  14.1 0.0 copy-done.2
  14.1 0.8 fusion.2
  14.9 0.1 reshape.28
  15.0 16.1 %fusion.8 = f32[4096,1024]{1,0:T(8,128)} fusion(f32[2,4096]{1,0:T(2,128)S(1)} %reshape.28, f32[2]{0:T(128)S(1)} %copy-done.2), kind=kOutput, calls=%fused_computation.12 | convolution fusion | flops 100671488 | bytes 16818688 | tf_op jit(solution)/shard_map/dot_general | solution.py:36
  31.1 0.0 reduce-scatter.2.cloned.1.call-update
  31.1 35.5 %psum.7 = f32[]{:T(128)} all-reduce(f32[]{:T(128)} %get-tuple-element.2), channel_id=1, replica_groups=mesh['groups'=2,'dp'=16] {'dp'}, use_global_device_ids=true, to_apply=%region_2.0 | all-reduce | flops 1 | bytes 8 | tf_op jit(solution)/shard_map/psum | solution.py:46
  66.7 0.6 convert_element_type.11
  68.0 144.5 %reduce-scatter.2.cloned.1.call-done = f32[256,1024]{1,0:T(8,128)} async-done(((f32[4096,1024]{1,0:T(8,128)}), f32[256,1024]{1,0:T(8,128)}) %reduce-scatter.2.cloned.1.call-update) | async-done | bytes 1048592 | tf_op jit(solution)/shard_map/reduce_scatter | solution.py:35
  212.5 2.3 %broadcast_multiply_fusion = f32[256,1024]{1,0:T(8,128)} fusion(f32[256,1024]{1,0:T(8,128)} %reduce-scatter.2.cloned.1.call-done, f32[]{:T(128)S(6)} %div.3), kind=kLoop, calls=%fused_computation.4 | loop fusion | flops 262144 | bytes 2097156 | tf_op jit(solution)/shard_map/mul | solution.py:47
Async XLA Ops:
  7.2 6.2 %copy-start = (bf16[2,128,4096]{2,1,0:T(8,128)(2,1)S(1)}, bf16[2,128,4096]{2,1,0:T(8,128)(2,1)}, u32[]{:S(2)}) copy-start(bf16[2,128,4096]{2,1,0:T(8,128)(2,1)} %param.6) | copy-start | bytes 6291460
  7.2 205.3 %reduce-scatter.2.cloned.1.call-start = ((), (), s32[]{:S(2)}) async-start(), calls=%async_computation.1 | async-start | bytes 17825792 | tf_op jit(solution)/shard_map/reduce_scatter | solution.py:35
  7.2 6.1 %copy-start.1 = (bf16[4096,64]{0,1:T(8,128)(2,1)S(1)}, bf16[4096,64]{0,1:T(8,128)(2,1)}, u32[]{:S(2)}) copy-start(bf16[4096,64]{0,1:T(8,128)(2,1)} %param.8) | copy-start | bytes 1572868
  13.3 0.8 copy-start.2
Sparse Core Ops, SparseCore 0:
  31.3 181.2 reduce-scatter.1
where the time goes:
time: 222 us
  waiting for transfers between devices  145 us (65%)
  blocking collectives  35.5 us (16%)
  matrix products  23.7 us (11%)
  between operations  14.8 us (7%)
  other arithmetic  2.92 us (1%)
    reduce_scatter x1, waiting for transfers between devices, local(): lax.psum_scatter(jnp.dot(weighted.T, left_cols, precision=lax.Precision.H...  145 us
    psum x1, blocking collectives, local(): trace_total = lax.psum(jnp.sum(weighted * flat), 'dp')  35.5 us
    dot_general x1, matrix products, local(): jnp.dot(weighted.T, left_cols, precision=lax.Precision.HIGHEST, preferred...  16.1 us
    dot_general x1, matrix products, local(): jnp.dot(stored_inputs.reshape(ex_count * seq_len, in_width), basis_in, pr...  6.08 us
  transfers between devices with their start and end apart: 1, of which 1 were waited for; matrix products, arithmetic and copies ran while one was open for 0% of the time, Pallas kernels for 0%

commit v1 on v0

v1 whole, which is shorter than its diff:
```python
import functools

import jax
import jax.numpy as jnp
from jax import lax
from jax.experimental import pallas as pl
from jax.experimental.pallas import tpu as pltpu
from jax.sharding import PartitionSpec as P

FCOLS = 1024
LANES = 128
EPSILON = 1e-6
NT = (((1,), (1,)), ((), ()))
TN = (((0,), (0,)), ((), ()))


def cut(total, most):
    tiles = total // LANES
    count = -(-total // most)
    edges = [tiles * i // count * LANES for i in range(count + 1)]
    return list(zip(edges[:-1], edges[1:]))


def split(value):
    high = value.astype(jnp.bfloat16)
    return high, (value - high.astype(jnp.float32)).astype(jnp.bfloat16)


def kernel(n, ex, own_rows, x_cuts, g_cuts, x_ref, g_ref, bi_ref, bo_ref, w_ref, fisher_ref, pg_ref,
           xv, gv, biv, bov, wv, blk, flatv, msg, recv, outv, pgv,
           xs, bis, gs, bos, send_sem, recv_sem, out_sem, pg_sem, w_sem):
    me = lax.axis_index("dp")
    tokens = x_ref.shape[0] // ex
    rank_in, rank_out = bi_ref.shape[0], bo_ref.shape[0]
    left = FCOLS // LANES
    flat_rows = rank_in * rank_out // LANES
    seg = max(1, own_rows // LANES)
    stat = ex * (left + seg)

    def load(ref, buf, sem, i, lo, hi):
        return pltpu.make_async_copy(ref.at[:, lo:hi], buf.at[:, lo:hi], sem.at[i])

    for i, (lo, hi) in enumerate(g_cuts):
        load(bo_ref, bov, bos, i, lo, hi).start()
        load(g_ref, gv, gs, i, lo, hi).start()
    for i, (lo, hi) in enumerate(x_cuts):
        load(bi_ref, biv, bis, i, lo, hi).start()
        load(x_ref, xv, xs, i, lo, hi).start()

    w_copy = pltpu.make_async_copy(w_ref, wv, w_sem)
    w_copy.start()

    barrier = pltpu.get_barrier_semaphore()
    for k in range(1, n):
        pl.semaphore_signal(barrier, inc=1, device_id={"dp": lax.rem(me + k, n)}, device_id_type=pl.DeviceIdType.MESH)

    def project(ref, buf, sem, b_ref, b_buf, b_sem, cuts):
        total = None
        for i, (lo, hi) in enumerate(cuts):
            load(b_ref, b_buf, b_sem, i, lo, hi).wait()
            load(ref, buf, sem, i, lo, hi).wait()
            term = lax.dot_general(buf[:, lo:hi], b_buf[:, lo:hi], NT, preferred_element_type=jnp.float32)
            total = term if total is None else total + term
        return total.astype(jnp.bfloat16)

    proj_out = project(g_ref, gv, gs, bo_ref, bov, bos, g_cuts)
    proj_in = project(x_ref, xv, xs, bi_ref, biv, bis, x_cuts)

    w_copy.wait()
    trace = None
    for e in range(ex):
        span = slice(e * tokens, (e + 1) * tokens)
        blk[e] = lax.dot_general(proj_out[span], proj_in[span], TN, preferred_element_type=jnp.float32)
    for e in range(ex):
        per = LANES // rank_in
        flat = jnp.concatenate([blk[e, pl.ds(p, flat_rows, per), :] for p in range(per)], axis=1)
        weighted = flat * wv[e]
        flatv[e] = flat
        term = jnp.sum(weighted * flat, axis=0, keepdims=True)
        trace = term if trace is None else trace + term
        for d in range(n):
            first = d * own_rows // LANES
            msg[d, e * left:(e + 1) * left] = flat[:left]
            msg[d, ex * left + e * seg:ex * left + (e + 1) * seg] = weighted[first:first + seg]
    for d in range(n):
        msg[d, stat:stat + 1] = trace

    pl.semaphore_wait(barrier, n - 1)

    def send(k):
        to = lax.rem(me + k, n)
        return pltpu.make_async_remote_copy(
            src_ref=msg.at[to], dst_ref=recv.at[me], send_sem=send_sem.at[k], recv_sem=recv_sem.at[me],
            device_id={"dp": to}, device_id_type=pl.DeviceIdType.MESH)

    def arrival(k):
        source = lax.rem(me + n - k, n)
        return pltpu.make_async_remote_copy(
            src_ref=msg.at[me], dst_ref=recv.at[source], send_sem=send_sem.at[k], recv_sem=recv_sem.at[source],
            device_id={"dp": source}, device_id_type=pl.DeviceIdType.MESH)

    for k in range(1, n):
        send(k).start()
    recv[me] = msg[me]
    for q in range(flat_rows):
        pgv[:, q * LANES:(q + 1) * LANES] = flatv[:, q, :].astype(jnp.bfloat16)
    pg_copy = pltpu.make_async_copy(pgv, pg_ref, pg_sem)
    pg_copy.start()
    for k in range(1, n):
        arrival(k).wait_recv()

    def rows(first, step):
        return jnp.concatenate([recv[:, first + e * step, :] for e in range(ex)], axis=0)

    total = jnp.sum(recv[:, stat, :], keepdims=True)
    scale = (rank_in * rank_out) / (total + EPSILON)
    lhs = jnp.concatenate([rows(ex * left + q, seg) for q in range(seg)], axis=1) * scale
    lhs_high, lhs_low = split(lhs)
    lhs = jnp.concatenate([lhs_high, lhs_high, lhs_low], axis=0)
    rhs_high, rhs_low = split(jnp.concatenate([rows(j, left) for j in range(left)], axis=1))
    rhs = jnp.concatenate([rhs_high, rhs_low, rhs_high], axis=0)
    copies = []
    if own_rows % LANES:
        outv[...] = lax.dot_general(lhs, rhs, TN, preferred_element_type=jnp.float32)
        first = pl.multiple_of(lax.rem(me * own_rows, LANES), own_rows)
        copies.append(pltpu.make_async_copy(outv.at[pl.ds(first, own_rows)], fisher_ref, out_sem.at[0]))
        copies[-1].start()
    else:
        for i in range(seg):
            span = slice(i * LANES, (i + 1) * LANES)
            outv[span] = lax.dot_general(lhs[:, span], rhs, TN, preferred_element_type=jnp.float32)
            copies.append(pltpu.make_async_copy(outv.at[span], fisher_ref.at[span], out_sem.at[i]))
            copies[-1].start()
    for k in range(1, n):
        send(k).wait_send()
    pg_copy.wait()
    for copy in copies:
        copy.wait()


def local(n, stored_inputs, output_grads, basis_in, basis_out, ex_weight):
    ex, seq, ff = stored_inputs.shape
    width = output_grads.shape[2]
    rank_in, rank_out = basis_in.shape[1], basis_out.shape[1]
    flat_width = rank_in * rank_out
    own_rows = flat_width // n
    seg = max(1, own_rows // LANES)
    x_cuts, g_cuts = cut(ff, 2048), cut(width, 2048)
    msg_rows = -(-(ex * (FCOLS // LANES + seg) + 1) // 8) * 8
    any_spec = pl.BlockSpec(memory_space=pl.ANY)
    bf16, f32 = jnp.bfloat16, jnp.float32
    dma = pltpu.SemaphoreType.DMA
    return pl.pallas_call(
        functools.partial(kernel, n, ex, own_rows, x_cuts, g_cuts),
        out_shape=(jax.ShapeDtypeStruct((own_rows, FCOLS), f32), jax.ShapeDtypeStruct((ex, flat_width), bf16)),
        in_specs=[pl.BlockSpec(memory_space=pltpu.HBM)] * 5,
        out_specs=(any_spec, any_spec),
        scratch_shapes=[
            pltpu.VMEM((ex * seq, ff), bf16),
            pltpu.VMEM((ex * seq, width), bf16),
            pltpu.VMEM((rank_in, ff), bf16),
            pltpu.VMEM((rank_out, width), bf16),
            pltpu.SMEM((ex,), f32),
            pltpu.VMEM((ex, rank_out, rank_in), f32),
            pltpu.VMEM((ex, flat_width // LANES, LANES), f32),
            pltpu.VMEM((n, msg_rows, LANES), f32),
            pltpu.VMEM((n, msg_rows, LANES), f32),
            pltpu.VMEM((seg * LANES, FCOLS), f32),
            pltpu.VMEM((ex, flat_width), bf16),
            dma((len(x_cuts),)), dma((len(x_cuts),)), dma((len(g_cuts),)), dma((len(g_cuts),)),
            dma((n,)), dma((n,)), dma((seg,)), dma(()), dma(()),
        ],
        compiler_params=pltpu.CompilerParams(
            collective_id=0, has_side_effects=True, vmem_limit_bytes=48 * 1024 * 1024),
    )(stored_inputs.reshape(ex * seq, ff), output_grads.reshape(ex * seq, width), basis_in.T, basis_out.T, ex_weight)


def solution(mesh):
    in_specs = (
        P(("groups", "dp"), None, None),
        P(("groups", "dp"), None, None),
        P(),
        P(),
        P(("groups", "dp")),
    )
    out_specs = (P(("groups", "dp"), None), P(("groups", "dp"), None))
    return jax.shard_map(functools.partial(local, mesh.shape["dp"]), mesh=mesh, in_specs=in_specs, out_specs=out_specs, check_vma=False)
```

time: 222 us -> 22.8 us (0.10)
  waiting for transfers between devices: 145 us -> 0 us
  blocking collectives: 35.5 us -> 0 us
  matrix products: 23.7 us -> 0 us
  Pallas kernels: 0 us -> 15.6 us
  between operations: 14.8 us -> 0.65 us
  local copies, waits for them, and re-layouts: 0.11 us -> 6.36 us
  other arithmetic: 2.92 us -> 0 us
    reduce_scatter x1 -> x0, waiting for transfers between devices: 145 us -> none  [local(): lax.psum_scatter(jnp.dot(weighted.T, left_cols, precision=lax.Precision.H...]
    psum x1 -> x0, blocking collectives: 35.5 us -> none  [local(): trace_total = lax.psum(jnp.sum(weighted * flat), 'dp')]
    dot_general x4 -> x0, matrix products: 23.7 us -> none  [the longest x1 16.1 us: local(): jnp.dot(weighted.T, left_cols, precision=lax.Precision.HIGHEST, preferred...]
    pallas_call x0 -> x1, Pallas kernels: none -> 15.6 us  [local(): pl.pallas_call(functools.partial(kernel, n, ex, own_rows, x_cuts, g_cuts)...]
    unnamed x6 -> x10, local copies, waits for them, and re-layouts: 0.02 us -> 6.36 us
    mul x1 -> x0, other arithmetic: 2.3 us -> none  [local(): fisher = fisher_rows * (proj_width / (trace_total + epsilon))]
  transfers between devices with their start and end apart: 1 -> 0, of which waited for: 1 -> 0; matrix products, arithmetic and copies ran while one was open for 0% -> 0% of each run, Pallas kernels for 0% -> 0%
where the time goes in v1:
time: 22.8 us; the launch traced here: 22.6 us
  Pallas kernels  15.6 us (68%)
  local copies, waits for them, and re-layouts  6.36 us (28%)
  between operations  0.65 us (3%)
    pallas_call x1, Pallas kernels, local(): pl.pallas_call(functools.partial(kernel, n, ex, own_rows, x_cuts, g_cuts)...  15.6 us
    unnamed x10, local copies, waits for them, and re-layouts  6.36 us

profile of v1, /device:TPU:0, one launch (start us, length us, event | category | flops | bytes accessed | tf_op | source)
XLA Modules:
  0.0 22.6 jit_solution(12797980899897094992)
XLA Ops:
  0.6 0.0 copy-start
  0.6 1.6 %copy-done = bf16[2,128,4096]{2,1,0:T(8,128)(2,1)S(1)} copy-done((bf16[2,128,4096]{2,1,0:T(8,128)(2,1)S(1)}, bf16[2,128,4096]{2,1,0:T(8,128)(2,1)}, u32[]{:S(2)}) %copy-start) | copy-done | bytes 2097176
  2.2 0.0 copy-start.1
  2.2 1.5 %copy-done.1 = bf16[14336,64]{0,1:T(8,128)(2,1)S(1)} copy-done((bf16[14336,64]{0,1:T(8,128)(2,1)S(1)}, bf16[14336,64]{0,1:T(8,128)(2,1)}, u32[]{:S(2)}) %copy-start.1) | copy-done | bytes 1835032
  3.7 0.0 copy-start.2
  3.7 1.0 %copy-done.2 = bf16[4096,64]{0,1:T(8,128)(2,1)S(1)} copy-done((bf16[4096,64]{0,1:T(8,128)(2,1)S(1)}, bf16[4096,64]{0,1:T(8,128)(2,1)}, u32[]{:S(2)}) %copy-start.2) | copy-done | bytes 524312
  4.8 0.0 copy-start.3
  4.8 0.7 %copy-done.3 = f32[2]{0:T(128)S(1)} copy-done((f32[2]{0:T(128)S(1)}, f32[2]{0:T(128)}, u32[]{:S(2)}) %copy-start.3) | copy-done | bytes 32
  5.4 15.6 %shard_map.68 = (f32[256,1024]{1,0:T(8,128)S(1)}, bf16[2,4096]{1,0:T(2,128)(2,1)S(1)}) custom-call(bf16[256,14336]{1,0:T(8,128)(2,1)} %bitcast.7, bf16[256,4096]{1,0:T(8,128)(2,1)S(1)} %bitcast.4, bf16[64,14336]{1,0:T(8,128)(2,1)S(1)} %bitcast.5, bf16[64,4096]{1,0:T(8,128)(2,1)S(1)} %bitcast.6, f32[2]{0:T(128)S(1)} %copy-done.3), custom_call_target="tpu_custom_call" | custom-call | tf_op jit(solution)/shard_map/pallas_call | solution.py:153
  21.0 1.0 %copy.9 = f32[256,1024]{1,0:T(8,128)} copy(f32[256,1024]{1,0:T(8,128)S(1)} %get-tuple-element.4) | data formatting | bytes 2097152
  22.0 0.6 %copy.10 = bf16[2,4096]{1,0:T(2,128)(2,1)} copy(bf16[2,4096]{1,0:T(2,128)(2,1)S(1)} %get-tuple-element.5) | data formatting | bytes 32768
Async XLA Ops:
  0.6 1.6 %copy-start = (bf16[2,128,4096]{2,1,0:T(8,128)(2,1)S(1)}, bf16[2,128,4096]{2,1,0:T(8,128)(2,1)}, u32[]{:S(2)}) copy-start(bf16[2,128,4096]{2,1,0:T(8,128)(2,1)} %param.6) | copy-start | bytes 6291460
  2.2 1.5 %copy-start.1 = (bf16[14336,64]{0,1:T(8,128)(2,1)S(1)}, bf16[14336,64]{0,1:T(8,128)(2,1)}, u32[]{:S(2)}) copy-start(bf16[14336,64]{0,1:T(8,128)(2,1)} %param.7) | copy-start | bytes 5505028
  3.7 1.0 %copy-start.2 = (bf16[4096,64]{0,1:T(8,128)(2,1)S(1)}, bf16[4096,64]{0,1:T(8,128)(2,1)}, u32[]{:S(2)}) copy-start(bf16[4096,64]{0,1:T(8,128)(2,1)} %param.8) | copy-start | bytes 1572868
  4.8 0.7 %copy-start.3 = (f32[2]{0:T(128)S(1)}, f32[2]{0:T(128)}, u32[]{:S(2)}) copy-start(f32[2]{0:T(128)} %w_ref.1) | copy-start | bytes 28

commit v2 on v1

--- a/solution.py
+++ b/solution.py
@@ -9,6 +9,7 @@
 
 FCOLS = 1024
 LANES = 128
+WINDOW = 4
 EPSILON = 1e-6
 NT = (((1,), (1,)), ((), ()))
 TN = (((0,), (0,)), ((), ()))
@@ -26,9 +27,9 @@
     return high, (value - high.astype(jnp.float32)).astype(jnp.bfloat16)
 
 
-def kernel(n, ex, own_rows, x_cuts, g_cuts, x_ref, g_ref, bi_ref, bo_ref, w_ref, fisher_ref, pg_ref,
-           xv, gv, biv, bov, wv, blk, flatv, msg, recv, outv, pgv,
-           xs, bis, gs, bos, send_sem, recv_sem, out_sem, pg_sem, w_sem):
+def exchange(n, ex, own_rows, x_cuts, g_cuts, x_ref, g_ref, bi_ref, bo_ref, w_ref, recv, pg_ref,
+           xv, gv, biv, bov, wv, blk, flatv, msg, pgv,
+           xs, bis, gs, bos, send_sem, recv_sem, own_sem, pg_sem, w_sem):
     me = lax.axis_index("dp")
     tokens = x_ref.shape[0] // ex
     rank_in, rank_out = bi_ref.shape[0], bo_ref.shape[0]
@@ -40,13 +41,17 @@
     def load(ref, buf, sem, i, lo, hi):
         return pltpu.make_async_copy(ref.at[:, lo:hi], buf.at[:, lo:hi], sem.at[i])
 
-    for i, (lo, hi) in enumerate(g_cuts):
-        load(bo_ref, bov, bos, i, lo, hi).start()
-        load(g_ref, gv, gs, i, lo, hi).start()
-    for i, (lo, hi) in enumerate(x_cuts):
-        load(bi_ref, biv, bis, i, lo, hi).start()
-        load(x_ref, xv, xs, i, lo, hi).start()
-
+    chunks = [((x_ref, xv, xs), (bi_ref, biv, bis), i, lo, hi) for i, (lo, hi) in enumerate(x_cuts)]
+    chunks += [((g_ref, gv, gs), (bo_ref, bov, bos), i, lo, hi) for i, (lo, hi) in enumerate(g_cuts)]
+
+    def issue(at):
+        if at < len(chunks):
+            data, basis, i, lo, hi = chunks[at]
+            load(*basis, i, lo, hi).start()
+            load(*data, i, lo, hi).start()
+
+    for at in range(WINDOW):
+        issue(at)
     w_copy = pltpu.make_async_copy(w_ref, wv, w_sem)
     w_copy.start()
 
@@ -54,17 +59,15 @@
     for k in range(1, n):
         pl.semaphore_signal(barrier, inc=1, device_id={"dp": lax.rem(me + k, n)}, device_id_type=pl.DeviceIdType.MESH)
 
-    def project(ref, buf, sem, b_ref, b_buf, b_sem, cuts):
-        total = None
-        for i, (lo, hi) in enumerate(cuts):
-            load(b_ref, b_buf, b_sem, i, lo, hi).wait()
-            load(ref, buf, sem, i, lo, hi).wait()
-            term = lax.dot_general(buf[:, lo:hi], b_buf[:, lo:hi], NT, preferred_element_type=jnp.float32)
-            total = term if total is None else total + term
-        return total.astype(jnp.bfloat16)
-
-    proj_out = project(g_ref, gv, gs, bo_ref, bov, bos, g_cuts)
-    proj_in = project(x_ref, xv, xs, bi_ref, biv, bis, x_cuts)
+    totals = {}
+    for at, (data, basis, i, lo, hi) in enumerate(chunks):
+        load(*basis, i, lo, hi).wait()
+        load(*data, i, lo, hi).wait()
+        issue(at + WINDOW)
+        term = lax.dot_general(data[1][:, lo:hi], basis[1][:, lo:hi], NT, preferred_element_type=jnp.float32)
+        side = "in" if at < len(x_cuts) else "out"
+        totals[side] = totals[side] + term if side in totals else term
+    proj_in, proj_out = (totals[side].astype(jnp.bfloat16) for side in ("in", "out"))
 
     w_copy.wait()
     trace = None
@@ -101,7 +104,8 @@
 
     for k in range(1, n):
         send(k).start()
-    recv[me] = msg[me]
+    own_copy = pltpu.make_async_copy(msg.at[me], recv.at[me], own_sem)
+    own_copy.start()
     for q in range(flat_rows):
         pgv[:, q * LANES:(q + 1) * LANES] = flatv[:, q, :].astype(jnp.bfloat16)
     pg_copy = pltpu.make_async_copy(pgv, pg_ref, pg_sem)
@@ -109,11 +113,24 @@
     for k in range(1, n):
         arrival(k).wait_recv()
 
+    for k in range(1, n):
+        send(k).wait_send()
+    own_copy.wait()
+    pg_copy.wait()
+
+
+def gram(n, ex, own_rows, flat_width, recv, pg_in, fisher_ref, pg_ref, outv, out_sem, pg_sem):
+    left = FCOLS // LANES
+    seg = max(1, own_rows // LANES)
+    stat = ex * (left + seg)
+    pg_copy = pltpu.make_async_copy(pg_in, pg_ref, pg_sem)
+    pg_copy.start()
+
     def rows(first, step):
         return jnp.concatenate([recv[:, first + e * step, :] for e in range(ex)], axis=0)
 
     total = jnp.sum(recv[:, stat, :], keepdims=True)
-    scale = (rank_in * rank_out) / (total + EPSILON)
+    scale = flat_width / (total + EPSILON)
     lhs = jnp.concatenate([rows(ex * left + q, seg) for q in range(seg)], axis=1) * scale
     lhs_high, lhs_low = split(lhs)
     lhs = jnp.concatenate([lhs_high, lhs_high, lhs_low], axis=0)
@@ -122,6 +139,7 @@
     copies = []
     if own_rows % LANES:
         outv[...] = lax.dot_general(lhs, rhs, TN, preferred_element_type=jnp.float32)
+        me = lax.axis_index("dp")
         first = pl.multiple_of(lax.rem(me * own_rows, LANES), own_rows)
         copies.append(pltpu.make_async_copy(outv.at[pl.ds(first, own_rows)], fisher_ref, out_sem.at[0]))
         copies[-1].start()
@@ -131,8 +149,6 @@
             outv[span] = lax.dot_general(lhs[:, span], rhs, TN, preferred_element_type=jnp.float32)
             copies.append(pltpu.make_async_copy(outv.at[span], fisher_ref.at[span], out_sem.at[i]))
             copies[-1].start()
-    for k in range(1, n):
-        send(k).wait_send()
     pg_copy.wait()
     for copy in copies:
         copy.wait()
@@ -150,10 +166,13 @@
     any_spec = pl.BlockSpec(memory_space=pl.ANY)
     bf16, f32 = jnp.bfloat16, jnp.float32
     dma = pltpu.SemaphoreType.DMA
-    return pl.pallas_call(
-        functools.partial(kernel, n, ex, own_rows, x_cuts, g_cuts),
-        out_shape=(jax.ShapeDtypeStruct((own_rows, FCOLS), f32), jax.ShapeDtypeStruct((ex, flat_width), bf16)),
-        in_specs=[pl.BlockSpec(memory_space=pltpu.HBM)] * 5,
+    vmem_spec = pl.BlockSpec(memory_space=pltpu.VMEM)
+    flat_grads = jax.ShapeDtypeStruct((ex, flat_width), bf16)
+    operands = (stored_inputs.reshape(ex * seq, ff), output_grads.reshape(ex * seq, width), basis_in.T, basis_out.T, ex_weight)
+    recv, grads = pl.pallas_call(
+        functools.partial(exchange, n, ex, own_rows, x_cuts, g_cuts),
+        out_shape=(jax.ShapeDtypeStruct((n, msg_rows, LANES), f32), flat_grads),
+        in_specs=[any_spec] * 5,
         out_specs=(any_spec, any_spec),
         scratch_shapes=[
             pltpu.VMEM((ex * seq, ff), bf16),
@@ -164,15 +183,21 @@
             pltpu.VMEM((ex, rank_out, rank_in), f32),
             pltpu.VMEM((ex, flat_width // LANES, LANES), f32),
             pltpu.VMEM((n, msg_rows, LANES), f32),
-            pltpu.VMEM((n, msg_rows, LANES), f32),
-            pltpu.VMEM((seg * LANES, FCOLS), f32),
             pltpu.VMEM((ex, flat_width), bf16),
             dma((len(x_cuts),)), dma((len(x_cuts),)), dma((len(g_cuts),)), dma((len(g_cuts),)),
-            dma((n,)), dma((n,)), dma((seg,)), dma(()), dma(()),
+            dma((n,)), dma((n,)), dma(()), dma(()), dma(()),
         ],
         compiler_params=pltpu.CompilerParams(
-            collective_id=0, has_side_effects=True, vmem_limit_bytes=48 * 1024 * 1024),
-    )(stored_inputs.reshape(ex * seq, ff), output_grads.reshape(ex * seq, width), basis_in.T, basis_out.T, ex_weight)
+            collective_id=0, has_side_effects=True, vmem_limit_bytes=40 * 1024 * 1024),
+    )(*(pltpu.with_memory_space_constraint(operand, pltpu.HBM) for operand in operands))
+    return pl.pallas_call(
+        functools.partial(gram, n, ex, own_rows, flat_width),
+        out_shape=(jax.ShapeDtypeStruct((own_rows, FCOLS), f32), flat_grads),
+        in_specs=[vmem_spec, any_spec],
+        out_specs=(any_spec, any_spec),
+        scratch_shapes=[pltpu.VMEM((seg * LANES, FCOLS), f32), dma((seg,)), dma(())],
+        compiler_params=pltpu.CompilerParams(vmem_limit_bytes=16 * 1024 * 1024),
+    )(recv, grads)
 
 
 def solution(mesh):

time: 22.8 us -> 17.9 us (0.79)
  local copies, waits for them, and re-layouts: 6.36 us -> 0 us
  Pallas kernels: 15.6 us -> 17.1 us
    unnamed x10 -> x0, local copies, waits for them, and re-layouts: 6.36 us -> none
    pallas_call x1 -> x2, Pallas kernels: 15.6 us -> 17.1 us  [the longest x1 15.7 us: local(): pl.pallas_call(functools.partial(exchange, n, ex, own_rows, x_cuts, g_cut...]
where the time goes in v2:
time: 17.9 us; the launch traced here: 17.7 us
  Pallas kernels  17.1 us (96%)
  between operations  0.64 us (4%)
    pallas_call x1, Pallas kernels, local(): pl.pallas_call(functools.partial(exchange, n, ex, own_rows, x_cuts, g_cut...  15.7 us
    pallas_call x1, Pallas kernels, local(): pl.pallas_call(functools.partial(gram, n, ex, own_rows, flat_width), out_...  1.38 us

profile of v2, /device:TPU:0, one launch (start us, length us, event | category | flops | bytes accessed | tf_op | source)
XLA Modules:
  0.0 17.7 jit_solution(1724022003382830221)
XLA Ops:
  0.6 15.7 %shard_map.68 = (f32[16,24,128]{2,1,0:T(8,128)S(1)}, bf16[2,4096]{1,0:T(2,128)(2,1)S(1)}) custom-call(bf16[256,14336]{1,0:T(8,128)(2,1)} %bitcast.4, bf16[256,4096]{1,0:T(8,128)(2,1)} %bitcast.5, bf16[64,14336]{1,0:T(8,128)(2,1)} %bitcast.6, bf16[64,4096]{1,0:T(8,128)(2,1)} %bitcast.7, f32[2]{0:T(128)} %w_ref.1), custom_call_target="tpu_custom_call" | custom-call | tf_op jit(solution)/shard_map/pallas_call | solution.py:172
  16.3 1.4 %shard_map.69 = (f32[256,1024]{1,0:T(8,128)}, bf16[2,4096]{1,0:T(2,128)(2,1)}) custom-call(f32[16,24,128]{2,1,0:T(8,128)S(1)} %get-tuple-element.4.recv, bf16[2,4096]{1,0:T(2,128)(2,1)S(1)} %get-tuple-element.5.pg_in), custom_call_target="tpu_custom_call" | custom-call | tf_op jit(solution)/shard_map/pallas_call | solution.py:193

commit v3 on v2

--- a/solution.py
+++ b/solution.py
@@ -9,26 +9,20 @@
 
 FCOLS = 1024
 LANES = 128
+CHUNK = 2048
 WINDOW = 4
 EPSILON = 1e-6
 NT = (((1,), (1,)), ((), ()))
 TN = (((0,), (0,)), ((), ()))
 
 
-def cut(total, most):
-    tiles = total // LANES
-    count = -(-total // most)
-    edges = [tiles * i // count * LANES for i in range(count + 1)]
-    return list(zip(edges[:-1], edges[1:]))
-
-
 def split(value):
     high = value.astype(jnp.bfloat16)
     return high, (value - high.astype(jnp.float32)).astype(jnp.bfloat16)
 
 
 def exchange(n, ex, own_rows, x_cuts, g_cuts, x_ref, g_ref, bi_ref, bo_ref, w_ref, recv, pg_ref,
-           xv, gv, biv, bov, wv, blk, flatv, msg, pgv,
+           xv, gv, biv, bov, wv, pv, blk, flatv, msg, pgv,
            xs, bis, gs, bos, send_sem, recv_sem, own_sem, pg_sem, w_sem):
     me = lax.axis_index("dp")
     tokens = x_ref.shape[0] // ex
@@ -38,42 +32,59 @@
     seg = max(1, own_rows // LANES)
     stat = ex * (left + seg)
 
-    def load(ref, buf, sem, i, lo, hi):
-        return pltpu.make_async_copy(ref.at[:, lo:hi], buf.at[:, lo:hi], sem.at[i])
-
-    chunks = [((x_ref, xv, xs), (bi_ref, biv, bis), i, lo, hi) for i, (lo, hi) in enumerate(x_cuts)]
-    chunks += [((g_ref, gv, gs), (bo_ref, bov, bos), i, lo, hi) for i, (lo, hi) in enumerate(g_cuts)]
+    x_set, g_set = ((x_ref, xv, xs), (bi_ref, biv, bis)), ((g_ref, gv, gs), (bo_ref, bov, bos))
+
+    def span_of(at):
+        return pl.ds(pl.multiple_of(at * CHUNK, CHUNK), CHUNK)
+
+    def load(ref, buf, sem, at):
+        return pltpu.make_async_copy(ref.at[:, span_of(at)], buf.at[:, span_of(at)], sem.at[at])
 
     def issue(at):
-        if at < len(chunks):
-            data, basis, i, lo, hi = chunks[at]
-            load(*basis, i, lo, hi).start()
-            load(*data, i, lo, hi).start()
-
-    for at in range(WINDOW):
-        issue(at)
+        for pair, first, last in ((x_set, 0, x_cuts), (g_set, x_cuts, x_cuts + g_cuts)):
+            @pl.when((at >= first) & (at < last))
+            def _():
+                load(*pair[1], at - first).start()
+                load(*pair[0], at - first).start()
+
+    def each(first, last, body):
+        def step(at, carry):
+            body(at)
+            return carry
+        lax.fori_loop(first, last, step, 0)
+
+    each(0, WINDOW, issue)
     w_copy = pltpu.make_async_copy(w_ref, wv, w_sem)
     w_copy.start()
 
     barrier = pltpu.get_barrier_semaphore()
-    for k in range(1, n):
+
+    @functools.partial(each, 1, n)
+    def _(k):
         pl.semaphore_signal(barrier, inc=1, device_id={"dp": lax.rem(me + k, n)}, device_id_type=pl.DeviceIdType.MESH)
 
-    totals = {}
-    for at, (data, basis, i, lo, hi) in enumerate(chunks):
-        load(*basis, i, lo, hi).wait()
-        load(*data, i, lo, hi).wait()
-        issue(at + WINDOW)
-        term = lax.dot_general(data[1][:, lo:hi], basis[1][:, lo:hi], NT, preferred_element_type=jnp.float32)
-        side = "in" if at < len(x_cuts) else "out"
-        totals[side] = totals[side] + term if side in totals else term
-    proj_in, proj_out = (totals[side].astype(jnp.bfloat16) for side in ("in", "out"))
+    def project(pair, first, count, slot):
+        (_, data, _), (_, basis, _) = pair
+
+        def step(at, total):
+            load(*pair[1], at).wait()
+            load(*pair[0], at).wait()
+            issue(first + at + WINDOW)
+            return total + lax.dot_general(
+                basis[:, span_of(at)], data[:, span_of(at)], NT, preferred_element_type=jnp.float32)
+
+        total = lax.fori_loop(0, count, step, jnp.zeros((basis.shape[0], data.shape[0]), jnp.float32))
+        pv[slot, :basis.shape[0]] = total.astype(jnp.bfloat16)
+
+    project(x_set, 0, x_cuts, 0)
+    project(g_set, x_cuts, g_cuts, 1)
 
     w_copy.wait()
+    pl.semaphore_wait(barrier, n - 1)
     trace = None
     for e in range(ex):
         span = slice(e * tokens, (e + 1) * tokens)
-        blk[e] = lax.dot_general(proj_out[span], proj_in[span], TN, preferred_element_type=jnp.float32)
+        blk[e] = lax.dot_general(pv[1, :rank_out, span], pv[0, :rank_in, span], NT, preferred_element_type=jnp.float32)
     for e in range(ex):
         per = LANES // rank_in
         flat = jnp.concatenate([blk[e, pl.ds(p, flat_rows, per), :] for p in range(per)], axis=1)
@@ -88,7 +99,6 @@
     for d in range(n):
         msg[d, stat:stat + 1] = trace
 
-    pl.semaphore_wait(barrier, n - 1)
 
     def send(k):
         to = lax.rem(me + k, n)
@@ -102,19 +112,16 @@
             src_ref=msg.at[me], dst_ref=recv.at[source], send_sem=send_sem.at[k], recv_sem=recv_sem.at[source],
             device_id={"dp": source}, device_id_type=pl.DeviceIdType.MESH)
 
-    for k in range(1, n):
-        send(k).start()
+    each(1, n, lambda k: send(k).start())
     own_copy = pltpu.make_async_copy(msg.at[me], recv.at[me], own_sem)
     own_copy.start()
     for q in range(flat_rows):
         pgv[:, q * LANES:(q + 1) * LANES] = flatv[:, q, :].astype(jnp.bfloat16)
     pg_copy = pltpu.make_async_copy(pgv, pg_ref, pg_sem)
     pg_copy.start()
-    for k in range(1, n):
-        arrival(k).wait_recv()
-
-    for k in range(1, n):
-        send(k).wait_send()
+    each(1, n, lambda k: arrival(k).wait_recv())
+
+    each(1, n, lambda k: send(k).wait_send())
     own_copy.wait()
     pg_copy.wait()
 
@@ -161,7 +168,7 @@
     flat_width = rank_in * rank_out
     own_rows = flat_width // n
     seg = max(1, own_rows // LANES)
-    x_cuts, g_cuts = cut(ff, 2048), cut(width, 2048)
+    x_cuts, g_cuts = ff // CHUNK, width // CHUNK
     msg_rows = -(-(ex * (FCOLS // LANES + seg) + 1) // 8) * 8
     any_spec = pl.BlockSpec(memory_space=pl.ANY)
     bf16, f32 = jnp.bfloat16, jnp.float32
@@ -180,11 +187,12 @@
             pltpu.VMEM((rank_in, ff), bf16),
             pltpu.VMEM((rank_out, width), bf16),
             pltpu.SMEM((ex,), f32),
+            pltpu.VMEM((2, max(rank_in, rank_out), ex * seq), bf16),
             pltpu.VMEM((ex, rank_out, rank_in), f32),
             pltpu.VMEM((ex, flat_width // LANES, LANES), f32),
             pltpu.VMEM((n, msg_rows, LANES), f32),
             pltpu.VMEM((ex, flat_width), bf16),
-            dma((len(x_cuts),)), dma((len(x_cuts),)), dma((len(g_cuts),)), dma((len(g_cuts),)),
+            dma((x_cuts,)), dma((x_cuts,)), dma((g_cuts,)), dma((g_cuts,)),
             dma((n,)), dma((n,)), dma(()), dma(()), dma(()),
         ],
         compiler_params=pltpu.CompilerParams(

time: 17.9 us -> 16.6 us (0.927)
  Pallas kernels: 17.1 us -> 15.8 us
    pallas_call x1, Pallas kernels: 15.7 us -> 14.4 us  [local(): pl.pallas_call(functools.partial(exchange, n, ex, own_rows, x_cuts, g_cut...]
where the time goes in v3:
time: 16.6 us; the launch traced here: 16.4 us
  Pallas kernels  15.8 us (95%)
  between operations  0.64 us (4%)
    pallas_call x1, Pallas kernels, local(): pl.pallas_call(functools.partial(exchange, n, ex, own_rows, x_cuts, g_cut...  14.4 us
    pallas_call x1, Pallas kernels, local(): pl.pallas_call(functools.partial(gram, n, ex, own_rows, flat_width), out_...  1.38 us

profile of v3, /device:TPU:0, one launch (start us, length us, event | category | flops | bytes accessed | tf_op | source)
XLA Modules:
  0.0 16.4 jit_solution(8685699218982813784)
XLA Ops:
  0.6 14.4 %shard_map.68 = (f32[16,24,128]{2,1,0:T(8,128)S(1)}, bf16[2,4096]{1,0:T(2,128)(2,1)S(1)}) custom-call(bf16[256,14336]{1,0:T(8,128)(2,1)} %bitcast.4, bf16[256,4096]{1,0:T(8,128)(2,1)} %bitcast.5, bf16[64,14336]{1,0:T(8,128)(2,1)} %bitcast.6, bf16[64,4096]{1,0:T(8,128)(2,1)} %bitcast.7, f32[2]{0:T(128)} %w_ref.1), custom_call_target="tpu_custom_call" | custom-call | tf_op jit(solution)/shard_map/pallas_call | solution.py:179
  15.0 1.4 %shard_map.69 = (f32[256,1024]{1,0:T(8,128)}, bf16[2,4096]{1,0:T(2,128)(2,1)}) custom-call(f32[16,24,128]{2,1,0:T(8,128)S(1)} %get-tuple-element.4.recv, bf16[2,4096]{1,0:T(2,128)(2,1)S(1)} %get-tuple-element.5.pg_in), custom_call_target="tpu_custom_call" | custom-call | tf_op jit(solution)/shard_map/pallas_call | solution.py:201
